TPU v7x, 32 devices: a whole 2x2x4 slice. The times are simulated.
32 devices in a mesh: groups: 2 (over x), tile: 16 (over z, y, core).
Axes of the slice: x: 2, y: 2, z: 4, core: 2. Of those that a mesh axis runs over, the one named last changes fastest.
Arguments:
- strain: bfloat16 [12288, 2, 4096], P(('groups', 'tile')), parts along dimension 0, may hold values from -6 to 6
- tile_pairs: int32 [96, 2], P(('groups', 'tile')), parts along dimension 0, may hold values from 0 to 47, as said below
- tile_count: int32 [32], P(('groups', 'tile')), parts along dimension 0, may hold values from 2 to 3, as said below
Outputs:
- correlations: bfloat16 [96, 128, 8192], P(('groups', 'tile')), parts along dimension 0
There are 2 independent parts, one for each index of `groups`. A program takes and returns all parts, laid end to end along the dimension named above; each array names one. Nothing has to cross between parts.
Inputs may be any that keep to these rules, and one draw needn't show every extreme that they name: `tile_pairs`: row k holds row block k and a column block from k to k + 6; where k mod 3 is 0, the column block is k + 6, where it is 1, k + 3, or the last block where that lies beyond it. `tile_count`: some device has all 3 tiles live in every draw.
All inputs are finite; a program needn't handle non-finite values.
Results may differ from a plain program's by a relative error of at most 0.0075.
Values may be sent and summed in bfloat16 or wider, within the bound.
No kernel may reach another device: no remote copies, remote signals or barrier semaphores. Data moves between devices by JAX's collectives and lax.ppermute only.
A program may use at most 128 MiB of HBM per device.

v0:
```python
import functools
import math

import jax
import jax.numpy as jnp
import numpy as np
from jax import lax
from jax.experimental import pallas as pl
from jax.experimental.pallas import tpu as pltpu
from jax.sharding import PartitionSpec as P

CH = 128
WIN = 4096
BAND = 256
BIN0 = 60
SMOOTH = 64
LAGS = 64
FINE = 8
COARSE = LAGS // FINE
ROWS = 16
TOGETHER = 8
VMEM_BYTES = 60 * 2**20
BF16 = jnp.bfloat16
F32 = jnp.float32


def bin_order():
    return np.concatenate([np.arange(0, BAND, 2), np.arange(1, BAND, 2)])


def dft_tables():
    times = np.arange(WIN // 2, dtype=np.int64)[:, None]
    tables = []
    for parity in range(2):
        freqs = BIN0 + np.arange(parity, BAND, 2, dtype=np.int64)[None, :]
        angle = (times * freqs % WIN) * (2.0 * math.pi / WIN)
        tables.append(np.concatenate([np.cos(angle), -np.sin(angle)], 1))
    return np.stack(tables).astype(BF16)


def mean_table():
    group = bin_order() // SMOOTH
    return ((group[:, None] == group[None, :]) / SMOOTH).astype(BF16)


def fold_table(wins):
    inner = ROWS // wins
    row = np.arange(2 * inner * TOGETHER * wins)
    sign, s, c, w = np.unravel_index(row, (2, inner, TOGETHER, wins))
    table = np.zeros((row.size, row.size), np.float32)
    for half in range(2):
        column = np.ravel_multi_index((c, half + 0 * c, s, w), (TOGETHER, 2, inner, wins))
        table[row, column] = np.where((sign == 1) & (half == 1), -1.0, 1.0)
    return table.astype(BF16)


def phase_tables(scale):
    freqs = (BIN0 + bin_order())[None, :]
    coarse = FINE * np.arange(1, COARSE // 2 + 1)[:, None]
    fine = np.arange(FINE)[:, None]
    step = 2.0 * math.pi / WIN
    a = np.concatenate([np.cos(coarse * freqs * step), np.sin(coarse * freqs * step)], 1) * scale
    b = np.concatenate([np.cos(fine * freqs * step), np.sin(fine * freqs * step)], 1)
    return a.astype(np.float32), b.astype(np.float32)


def transform(x_ref, fold_ref, mean_ref, tab_ref, left, acc, wide, m, put):
    wins = ROWS // 8
    for pair in range(0, CH // TOGETHER, 2):
        sides = []
        for g in (pair, pair + 1):
            rows = x_ref[g * TOGETHER : (g + 1) * TOGETHER, :, 0]
            sides.append(rows.reshape(TOGETHER * 2 * ROWS, 128))
        folded = jnp.dot(
            fold_ref[...], jnp.concatenate(sides, 1), preferred_element_type=F32
        ).astype(BF16)
        size = TOGETHER * wins
        for sign in range(2):
            for s in range(8):
                piece = folded[(sign * 8 + s) * size : (sign * 8 + s + 1) * size]
                for n, g in enumerate((pair, pair + 1)):
                    left[sign, g * size : (g + 1) * size, s * 128 : (s + 1) * 128] = piece[
                        :, n * 128 : (n + 1) * 128
                    ]
    parts = [
        jnp.dot(left[sign], tab_ref[sign], preferred_element_type=F32) for sign in range(2)
    ]

    @pl.when(m == 0)
    def _():
        for sign in range(2):
            acc[sign] = parts[sign]

    @pl.when(m == 1)
    def _():
        spec = [acc[sign] + parts[sign] for sign in range(2)]
        energy = [s[:, :128] * s[:, :128] + s[:, 128:] * s[:, 128:] for s in spec]
        energy = jnp.concatenate(energy, 1)
        high = energy.astype(BF16)
        low = (energy - high.astype(F32)).astype(BF16)
        power = jnp.dot(high, mean_ref[...], preferred_element_type=F32)
        power += jnp.dot(low, mean_ref[...], preferred_element_type=F32)
        factor = lax.rsqrt(power + 1e-06)
        for sign in range(2):
            scaled = factor[:, sign * 128 : (sign + 1) * 128]
            wide[sign] = spec[sign][:, :128] * scaled
            wide[2 + sign] = spec[sign][:, 128:] * scaled
        for w in range(wins):
            for q in range(4):
                column = (w * 4 + q) * 128
                put(column, wide[q, pl.ds(w, CH, stride=wins), :].astype(BF16))


def first_kernel(x_ref, fold_ref, mean_ref, tab_ref, out_ref, left, acc, wide):
    def put(column, value):
        out_ref[:, column : column + 128] = value

    transform(x_ref, fold_ref, mean_ref, tab_ref, left, acc, wide, pl.program_id(1), put)


def rest_kernel(x_ref, fold_ref, mean_ref, tab_ref, w0_ref, one_ref, all_ref, left, acc, wide):
    block = pl.program_id(0)

    @pl.when(jnp.logical_and(block == 0, pl.program_id(1) == 0))
    def _():
        all_ref[0] = w0_ref[...]

    def put(column, value):
        all_ref[block + 1, :, column : column + 128] = value

        @pl.when(block == 0)
        def _():
            one_ref[:, column : column + 128] = value

    transform(x_ref, fold_ref, mean_ref, tab_ref, left, acc, wide, pl.program_id(1), put)


def spectra(kernel, view, consts, first, count, extra, outs, name):
    wins = ROWS // 8
    depth = WIN // 4
    whole = pl.BlockSpec(memory_space=pltpu.VMEM)
    return pl.pallas_call(
        kernel,
        grid=(count, 2),
        out_shape=[jax.ShapeDtypeStruct(shape, BF16) for shape in outs],
        in_specs=[
            pl.BlockSpec((CH, 2, 1, ROWS, 128), lambda b, m: (first + b, 0, m, 0, 0)),
            pl.BlockSpec((256, 256), lambda b, m: (0, 0)),
            pl.BlockSpec((BAND, BAND), lambda b, m: (0, 0)),
            pl.BlockSpec((2, depth, BAND), lambda b, m: (0, m, 0)),
        ]
        + [whole] * len(extra),
        out_specs=[whole] * len(outs),
        scratch_shapes=[
            pltpu.VMEM((2, CH * wins, depth), BF16),
            pltpu.VMEM((2, CH * wins, BAND), F32),
            pltpu.VMEM((4, CH * wins, 128), F32),
        ],
        compiler_params=pltpu.CompilerParams(vmem_limit_bytes=VMEM_BYTES),
        cost_estimate=pl.CostEstimate(
            flops=count * 4 * CH * wins * WIN * BAND,
            bytes_accessed=count * (2 * CH * wins * WIN + 2 * WIN * BAND),
            transcendentals=0,
        ),
        name=name,
    )(view, *consts, *extra)


def pick_kernel(blocks, want_ref, all_ref, other_ref, out_ref, sem):
    me = lax.axis_index("tile")
    index = want_ref[blocks - 1, 1] - me * blocks

    @pl.when(jnp.logical_or(index >= 0, me % 2 == 0))
    def _():
        copy = pltpu.make_async_copy(all_ref.at[jnp.clip(index, 0, blocks - 1)], out_ref, sem)
        copy.start()
        copy.wait()

    @pl.when(jnp.logical_and(index < 0, me % 2 == 1))
    def _():
        index2 = jnp.clip(index + blocks, 0, blocks - 1)
        copy = pltpu.make_async_copy(other_ref.at[index2], out_ref, sem)
        copy.start()
        copy.wait()


def pick(want, everything, other):
    blocks = everything.shape[0]
    return pl.pallas_call(
        functools.partial(pick_kernel, blocks),
        out_shape=jax.ShapeDtypeStruct(everything.shape[1:], BF16),
        in_specs=[
            pl.BlockSpec(memory_space=pltpu.SMEM),
            pl.BlockSpec(memory_space=pl.ANY),
            pl.BlockSpec(memory_space=pl.ANY),
        ],
        out_specs=pl.BlockSpec(memory_space=pltpu.VMEM),
        scratch_shapes=[pltpu.SemaphoreType.DMA],
        name="chosen_block",
    )(want, everything, other)


def corr_kernel(slot, blocks, scale, *refs):
    pairs_ref, count_ref, row_ref, atab_ref, btab_ref, all_ref, other_ref, far_ref = refs[:8]
    out_hbm, raw, col, acoef, b0, b1, p0, p1, obuf, in_sem, out_sem = refs[-11:]
    js = 256 // FINE
    chunks = CH // js
    live = count_ref[0] > slot
    me = lax.axis_index("tile")
    index = pairs_ref[slot, 1] - me * blocks
    even = me % 2 == 0
    own = index < blocks
    beside = jnp.logical_and(index >= blocks, jnp.logical_and(even, index < 2 * blocks))
    remote = jnp.logical_not(jnp.logical_or(own, beside))

    def out_copy(c):
        columns = pl.ds(c * js * LAGS, js * LAGS)
        return pltpu.make_async_copy(
            obuf.at[:, columns], out_hbm.at[slot, :, columns], out_sem.at[c]
        )

    @pl.when(live)
    def _():
        @pl.when(own)
        def _():
            pltpu.make_async_copy(all_ref.at[jnp.clip(index, 0, blocks - 1)], raw, in_sem).start()

        @pl.when(beside)
        def _():
            pltpu.make_async_copy(
                other_ref.at[jnp.clip(index - blocks, 0, blocks - 1)], raw, in_sem
            ).start()

        @pl.when(remote)
        def _():
            pltpu.make_async_copy(far_ref, raw, in_sem).start()

        for w in range(2):
            for p in range(2):
                re_cols = slice((w * 4 + p) * 128, (w * 4 + p + 1) * 128)
                im_cols = slice((w * 4 + 2 + p) * 128, (w * 4 + 3 + p) * 128)
                re = row_ref[0, :, re_cols].astype(F32)
                im = row_ref[0, :, im_cols].astype(F32)

                def put(a, re_value, im_value):
                    rows = slice(a * CH, (a + 1) * CH)
                    acoef[rows, re_cols] = re_value.astype(BF16)
                    acoef[rows, im_cols] = im_value.astype(BF16)

                middle = COARSE // 2
                put(middle, re * scale, im * scale)
                for n in range(1, middle + 1):
                    cos = atab_ref[n - 1 : n, p * 128 : (p + 1) * 128]
                    sin = atab_ref[n - 1 : n, (2 + p) * 128 : (3 + p) * 128]
                    rc, ic, rs, ims = re * cos, im * cos, re * sin, im * sin
                    put(middle - n, rc + ims, ic - rs)
                    if n < middle:
                        put(middle + n, rc - ims, ic + rs)
        pltpu.make_async_copy(far_ref, raw, in_sem).wait()
        for q in range(8):
            col[q] = raw[:, q * 128 : (q + 1) * 128].astype(F32)

        def build(c, b):
            for w in range(2):
                for p in range(2):
                    re_q, im_q = w * 4 + p, w * 4 + 2 + p
                    cos = btab_ref[:, p * 128 : (p + 1) * 128]
                    sin = btab_ref[:, (2 + p) * 128 : (3 + p) * 128]
                    for place in range(0, js, 2):
                        res, ims = [], []
                        for pos in (place, place + 1):
                            v, inner = divmod(pos, 16)
                            jj, q = divmod(inner, 8)
                            j = c * js + v * 16 + 2 * q + jj
                            re = col[re_q, pl.ds(j, FINE, stride=0), :]
                            im = col[im_q, pl.ds(j, FINE, stride=0), :]
                            res.append(re * cos + im * sin)
                            ims.append(im * cos - re * sin)
                        rows = slice(place * FINE, (place + 2) * FINE)
                        b[rows, re_q * 128 : (re_q + 1) * 128] = jnp.concatenate(res, 0).astype(BF16)
                        b[rows, im_q * 128 : (im_q + 1) * 128] = jnp.concatenate(ims, 0).astype(BF16)

        def multiply(b, p):
            p[...] = lax.dot_general(
                acoef[...], b[...], (((1,), (1,)), ((), ())), preferred_element_type=F32
            ).astype(BF16)

        lane = lax.broadcasted_iota(jnp.int32, (CH, 128), 1)

        def arrange(c, prod):
            for v in range(2):
                x = [prod[a * CH : (a + 1) * CH, v * 128 : (v + 1) * 128] for a in range(COARSE)]
                for bit in (1, 2, 4):
                    upper = (lane // FINE) & bit != 0
                    for a in range(COARSE):
                        if a & bit == 0:
                            lo, hi = x[a], x[a | bit]
                            x[a] = jnp.where(upper, pltpu.roll(hi, FINE * bit, 1), lo)
                            x[a | bit] = jnp.where(upper, hi, pltpu.roll(lo, 128 - FINE * bit, 1))
                for q in range(8):
                    column = c * js * LAGS + v * 1024 + q * 128
                    obuf[:, column : column + 128] = x[q]
            out_copy(c).start()

        bs, ps = (b0, b1), (p0, p1)
        build(0, b0)
        for c in range(chunks):
            multiply(bs[c % 2], ps[c % 2])
            if c + 1 < chunks:
                build(c + 1, bs[(c + 1) % 2])
            if c > 0:
                arrange(c - 1, ps[(c - 1) % 2])
        arrange(chunks - 1, ps[(chunks - 1) % 2])

    @pl.when(jnp.logical_not(live))
    def _():
        obuf[...] = jnp.zeros_like(obuf)
        for c in range(chunks):
            out_copy(c).start()

    for c in range(chunks):
        out_copy(c).wait()


def corr_tile(slot, scale, pairs, count, tables, everything, other, far, buffer):
    js = 256 // FINE
    chunks = CH // js
    blocks, _, depth = everything.shape
    in_specs = [
        pl.BlockSpec(memory_space=pltpu.SMEM),
        pl.BlockSpec(memory_space=pltpu.SMEM),
        pl.BlockSpec((1, CH, depth), lambda i: (slot, 0, 0)),
        pl.BlockSpec(memory_space=pltpu.VMEM),
        pl.BlockSpec(memory_space=pltpu.VMEM),
    ] + [pl.BlockSpec(memory_space=pl.ANY)] * 3
    operands = [pairs, count, everything, *tables, everything, other, far]
    aliases = {}
    if buffer is not None:
        aliases = {len(operands): 0}
        operands.append(buffer)
        in_specs.append(pl.BlockSpec(memory_space=pl.ANY))
    return pl.pallas_call(
        functools.partial(corr_kernel, slot, blocks, scale),
        grid=(1,),
        out_shape=jax.ShapeDtypeStruct((blocks, CH, CH * LAGS), BF16),
        in_specs=in_specs,
        out_specs=pl.BlockSpec(memory_space=pl.ANY),
        scratch_shapes=[
            pltpu.VMEM((CH, depth), BF16),
            pltpu.VMEM((8, CH, 128), F32),
            pltpu.VMEM((COARSE * CH, depth), BF16),
            pltpu.VMEM((js * FINE, depth), BF16),
            pltpu.VMEM((js * FINE, depth), BF16),
            pltpu.VMEM((COARSE * CH, js * FINE), BF16),
            pltpu.VMEM((COARSE * CH, js * FINE), BF16),
            pltpu.VMEM((CH, CH * LAGS), BF16),
            pltpu.SemaphoreType.DMA,
            pltpu.SemaphoreType.DMA((chunks,)),
        ],
        input_output_aliases=aliases,
        compiler_params=pltpu.CompilerParams(vmem_limit_bytes=VMEM_BYTES),
        cost_estimate=pl.CostEstimate(
            flops=4 * CH * CH * LAGS * depth, bytes_accessed=2 * CH * CH * LAGS, transcendentals=0
        ),
        name=f"lags_{slot}",
    )(*operands)


def body(strain, tile_pairs, tile_count):
    blocks = strain.shape[0] // CH
    wins = strain.shape[1]
    size = lax.axis_size("tile")
    depth = wins * 2 * BAND
    scale = 1.0 / math.sqrt(wins * BAND)
    consts = [jnp.asarray(t) for t in (fold_table(wins), mean_table(), dft_tables())]
    tables = [jnp.asarray(t) for t in phase_tables(scale)]
    ahead2 = [(i, i - 2) for i in range(2, size)]
    behind2 = [(i, i + 2) for i in range(size - 2)]
    across = [(i, i - 1) for i in range(2, size, 2)]
    swap = [(i, i ^ 1) for i in range(size)]

    view = strain.reshape(blocks * CH, wins, WIN // 128, 128).transpose(0, 2, 1, 3)
    view = view.reshape(blocks * CH, 2, 2, ROWS, 128)
    want = lax.ppermute(tile_pairs, "tile", behind2)
    (w0,) = spectra(first_kernel, view, consts, 0, 1, [], [(CH, depth)], "spectrum_0")
    far0 = lax.ppermute(w0, "tile", ahead2)
    w1, everything = spectra(
        rest_kernel, view, consts, 1, blocks - 1, [w0], [(CH, depth), (blocks, CH, depth)], "spectrum_rest"
    )
    near1 = lax.ppermute(w1, "tile", across)
    other = lax.ppermute(everything, "tile", swap)
    far2 = lax.ppermute(pick(want, everything, other), "tile", ahead2)
    out = None
    for slot, far in enumerate((far0, near1, far2)):
        out = corr_tile(
            slot, scale, tile_pairs, tile_count, tables, everything, other, far, out
        )
    return out


def solution(mesh):
    in_specs = (
        P(("groups", "tile"), None, None),
        P(("groups", "tile"), None),
        P(("groups", "tile")),
    )
    out_specs = P(("groups", "tile"), None, None)
    return jax.shard_map(body, mesh=mesh, in_specs=in_specs, out_specs=out_specs, check_vma=False)
```

profile of v0, /device:TPU:28, one launch (start us, length us, event | category | flops | bytes accessed | tf_op | source)
XLA Modules:
  0.0 52.2 jit_solution(11458360785747407465)
XLA Ops:
  0.0 4.2 %spectrum_0.1.w0_ref = bf16[128,1024]{1,0:T(8,128)(2,1)} custom-call(bf16[384,2,2,16,128]{4,3,2,1,0:T(8,128)(2,1)} %bitcast.5, bf16[256,256]{1,0:T(8,128)(2,1)} %constant.10.clone.fold_ref, bf16[256,256]{1,0:T(8,128)(2,1)} %constant.11.clone.mean_ref, bf16[2,2048,256]{2,1,0:T(8,128)(2,1)} %constant.12.clone.tab_ref), custom_call_target="tpu_custom_call" | custom-call | flops 1073741824 | bytes 4194304 | tf_op jit(solution)/shard_map/spectrum_0/pallas_call | solution.py:142
  4.2 0.0 copy-start
  4.2 0.0 copy-start.4
  4.2 7.5 %spectrum_rest.1 = (bf16[128,1024]{1,0:T(8,128)(2,1)}, bf16[3,128,1024]{2,1,0:T(8,128)(2,1)}) custom-call(bf16[384,2,2,16,128]{4,3,2,1,0:T(8,128)(2,1)} %bitcast.6, bf16[256,256]{1,0:T(8,128)(2,1)} %constant.10.clone.fold_ref, bf16[256,256]{1,0:T(8,128)(2,1)} %constant.11.clone.mean_ref, bf16[2,2048,256]{2,1,0:T(8,128)(2,1)} %constant.12.clone.tab_ref, ...), custom_call_target="tpu_custom_call" | custom-call | flops 2147483648 | bytes 8388608 | tf_op jit(solution)/shard_map/spectrum_rest/pallas_call | solution.py:142
  11.7 0.0 collective-permute-start
  11.7 0.0 copy-done
  11.7 2.4 %collective-permute-start.4 = (bf16[128,1024]{1,0:T(8,128)(2,1)S(1)}, bf16[128,1024]{1,0:T(8,128)(2,1)S(1)}, u32[]{:S(2)}, u32[]{:S(2)}) collective-permute-start(bf16[128,1024]{1,0:T(8,128)(2,1)S(1)} %copy-done), channel_id=1, source_target_pairs={{2,0},{3,1},{4,2},{5,3},{6,4},{7,5},{8,6},{9,7},{10,8},{11,9},{12,... | collective-permute-start | bytes 786440 | tf_op jit(solution)/shard_map/ppermute | solution.py:386
  14.2 3.1 %collective-permute-start.3 = (bf16[128,1024]{1,0:T(8,128)(2,1)}, bf16[128,1024]{1,0:T(8,128)(2,1)S(1)}, u32[]{:S(2)}, u32[]{:S(2)}) collective-permute-start(bf16[128,1024]{1,0:T(8,128)(2,1)} %get-tuple-element.8), channel_id=1, source_target_pairs={{2,1},{4,3},{6,5},{8,7},{10,9},{12,11},{14,13},{18,17},{20,19},{22... | collective-permute-start | bytes 786440 | tf_op jit(solution)/shard_map/ppermute | solution.py:390
  17.3 0.0 copy-done.4
  17.3 0.1 copy.15.refs_0_
  17.4 0.0 copy-start.2
  17.4 1.3 %collective-permute-start.1 = (s32[3,2]{1,0:T(4,128)S(1)}, s32[3,2]{1,0:T(4,128)S(1)}, u32[]{:S(2)}, u32[]{:S(2)}) collective-permute-start(s32[3,2]{1,0:T(4,128)S(1)} %copy.15.refs_0_), channel_id=1, source_target_pairs={{0,2},{1,3},{2,4},{3,5},{4,6},{5,7},{6,8},{7,9},{8,10},{9,11},{10,... | collective-permute-start | bytes 80 | tf_op jit(solution)/shard_map/ppermute | solution.py:384
  19.4 3.5 %collective-permute-done.1.want_ref = s32[3,2]{1,0:T(4,128)S(1)} collective-permute-done((s32[3,2]{1,0:T(4,128)S(1)}, s32[3,2]{1,0:T(4,128)S(1)}, u32[]{:S(2)}, u32[]{:S(2)}) %collective-permute-start.1) | collective-permute-done | bytes 56 | tf_op jit(solution)/shard_map/ppermute | solution.py:384
  22.9 0.0 copy-start.3
  22.9 0.0 collective-permute-done.other_ref.refs_6_
  22.9 0.6 %copy-done.3 = s32[3,2]{1,0:T(4,128)} copy-done((s32[3,2]{1,0:T(4,128)}, s32[3,2]{1,0:T(4,128)S(1)}, u32[]{:S(2)}) %copy-start.3) | copy-done | bytes 48
  23.5 0.9 %copy-done.1 = bf16[3,128,1024]{2,1,0:T(8,128)(2,1)} copy-done((bf16[3,128,1024]{2,1,0:T(8,128)(2,1)}, bf16[3,128,1024]{2,1,0:T(8,128)(2,1)S(1)}, u32[]{:S(2)}) %copy-start.1) | copy-done | bytes 786456
  24.4 2.4 %chosen_block.1 = bf16[128,1024]{1,0:T(8,128)(2,1)} custom-call(s32[3,2]{1,0:T(4,128)} %copy-done.3, bf16[3,128,1024]{2,1,0:T(8,128)(2,1)} %get-tuple-element.7.all_ref.refs_2_.refs_5_, bf16[3,128,1024]{2,1,0:T(8,128)(2,1)} %copy-done.1), custom_call_target="tpu_custom_call" | custom-call | tf_op jit(solution)/shard_map/chosen_block/pallas_call | solution.py:189
  26.8 3.4 %collective-permute-start.2 = (bf16[128,1024]{1,0:T(8,128)(2,1)}, bf16[128,1024]{1,0:T(8,128)(2,1)S(1)}, u32[]{:S(2)}, u32[]{:S(2)}) collective-permute-start(bf16[128,1024]{1,0:T(8,128)(2,1)} %chosen_block.1), channel_id=1, source_target_pairs={{2,0},{3,1},{4,2},{5,3},{6,4},{7,5},{8,6},{9,7},{10,8},{11,9},{12,... | collective-permute-start | bytes 786440 | tf_op jit(solution)/shard_map/ppermute | solution.py:392
  30.2 0.0 collective-permute-done.4.refs_7_
  30.2 0.0 copy-done.2
  30.2 0.0 copy-start.6
  30.2 0.7 %copy-done.6 = bf16[128,1024]{1,0:T(8,128)(2,1)} copy-done((bf16[128,1024]{1,0:T(8,128)(2,1)}, bf16[128,1024]{1,0:T(8,128)(2,1)S(1)}, u32[]{:S(2)}) %copy-start.6) | copy-done | bytes 262168
  30.9 6.5 %lags_0.1.refs_8_ = bf16[3,128,8192]{2,1,0:T(8,128)(2,1)} custom-call(s32[3,2]{1,0:T(4,128)} %copy-done.2, s32[1]{0:T(128)S(6)} %copy.18.refs_1_, bf16[3,128,1024]{2,1,0:T(8,128)(2,1)} %get-tuple-element.7.all_ref.refs_2_.refs_5_, f32[4,512]{1,0:T(4,128)} %constant.13.clone.refs_3_, f32[8,512]{1,0:T(8,128)} %constant.14.clone.refs_4_, ...), custom_call_target="tpu_custom_call" | custom-call | flops 4294967296 | bytes 2097152 | tf_op jit(solution)/shard_map/lags_0/pallas_call | solution.py:342
  37.4 0.0 collective-permute-done.3.refs_7_
  37.4 0.0 copy-start.5
  37.4 0.7 %copy-done.5 = bf16[128,1024]{1,0:T(8,128)(2,1)} copy-done((bf16[128,1024]{1,0:T(8,128)(2,1)}, bf16[128,1024]{1,0:T(8,128)(2,1)S(1)}, u32[]{:S(2)}) %copy-start.5) | copy-done | bytes 262168
  38.1 6.5 %lags_1.1.refs_8_ = bf16[3,128,8192]{2,1,0:T(8,128)(2,1)} custom-call(s32[3,2]{1,0:T(4,128)} %copy-done.2, s32[1]{0:T(128)S(6)} %copy.18.refs_1_, bf16[3,128,1024]{2,1,0:T(8,128)(2,1)} %get-tuple-element.7.all_ref.refs_2_.refs_5_, f32[4,512]{1,0:T(4,128)} %constant.13.clone.refs_3_, ...), custom_call_target="tpu_custom_call", output_to_operand_aliasing={{}: (8, {})} | custom-call | flops 4294967296 | bytes 2097152 | tf_op jit(solution)/shard_map/lags_1/pallas_call | solution.py:342
  44.6 0.0 collective-permute-done.2.refs_7_
  44.6 0.0 copy-start.7
  44.7 0.7 %copy-done.7 = bf16[128,1024]{1,0:T(8,128)(2,1)} copy-done((bf16[128,1024]{1,0:T(8,128)(2,1)}, bf16[128,1024]{1,0:T(8,128)(2,1)S(1)}, u32[]{:S(2)}) %copy-start.7) | copy-done | bytes 262168
  45.4 6.7 %lags_2.1 = bf16[3,128,8192]{2,1,0:T(8,128)(2,1)} custom-call(s32[3,2]{1,0:T(4,128)} %copy-done.2, s32[1]{0:T(128)S(6)} %copy.18.refs_1_, bf16[3,128,1024]{2,1,0:T(8,128)(2,1)} %get-tuple-element.7.all_ref.refs_2_.refs_5_, f32[4,512]{1,0:T(4,128)} %constant.13.clone.refs_3_, f32[8,512]{1,0:T(8,128)} %constant.14.clone.refs_4_, ...), custom_call_target="tpu_custom_call", output_to_operand_aliasing={{}: (8, {})} | custom-call | flops 4294967296 | bytes 2097152 | tf_op jit(solution)/shard_map/lags_2/pallas_call | solution.py:342
  (1 shorter events, 0.0 us)
Async XLA Ops:
  4.2 7.5 %copy-start = (bf16[128,1024]{1,0:T(8,128)(2,1)S(1)}, bf16[128,1024]{1,0:T(8,128)(2,1)}, u32[]{:S(2)}) copy-start(bf16[128,1024]{1,0:T(8,128)(2,1)} %spectrum_0.1.w0_ref) | copy-start | bytes 786436
  4.2 13.1 %copy-start.4 = (s32[3,2]{0,1:T(2,128)S(1)}, s32[3,2]{0,1:T(2,128)}, u32[]{:S(2)}) copy-start(s32[3,2]{0,1:T(2,128)} %param.9) | copy-start | bytes 76
  11.7 11.2 %collective-permute-start = (bf16[3,128,1024]{2,1,0:T(8,128)(2,1)}, bf16[3,128,1024]{2,1,0:T(8,128)(2,1)S(1)}, u32[]{:S(2)}, u32[]{:S(2)}) collective-permute-start(bf16[3,128,1024]{2,1,0:T(8,128)(2,1)} %get-tuple-element.7.all_ref.refs_2_.refs_5_), channel_id=1, source_target_pairs={{0,1},{1,0},{2,3},{3,2},{4,5},{5,4},{6,7},{7,6},{8,9},{9,8},{10,11... | collective-permute-start | bytes 2359304 | tf_op jit(solution)/shard_map/ppermute | solution.py:391
  11.7 18.5 %collective-permute-start.4 = (bf16[128,1024]{1,0:T(8,128)(2,1)S(1)}, bf16[128,1024]{1,0:T(8,128)(2,1)S(1)}, u32[]{:S(2)}, u32[]{:S(2)}) collective-permute-start(bf16[128,1024]{1,0:T(8,128)(2,1)S(1)} %copy-done), channel_id=1, source_target_pairs={{2,0},{3,1},{4,2},{5,3},{6,4},{7,5},{8,6},{9,7},{10,8},{11,9},{12,... | collective-permute-start | bytes 786440 | tf_op jit(solution)/shard_map/ppermute | solution.py:386
  14.2 23.2 %collective-permute-start.3 = (bf16[128,1024]{1,0:T(8,128)(2,1)}, bf16[128,1024]{1,0:T(8,128)(2,1)S(1)}, u32[]{:S(2)}, u32[]{:S(2)}) collective-permute-start(bf16[128,1024]{1,0:T(8,128)(2,1)} %get-tuple-element.8), channel_id=1, source_target_pairs={{2,1},{4,3},{6,5},{8,7},{10,9},{12,11},{14,13},{18,17},{20,19},{22... | collective-permute-start | bytes 786440 | tf_op jit(solution)/shard_map/ppermute | solution.py:390
  17.4 12.8 %copy-start.2 = (s32[3,2]{1,0:T(4,128)}, s32[3,2]{1,0:T(4,128)S(1)}, u32[]{:S(2)}) copy-start(s32[3,2]{1,0:T(4,128)S(1)} %copy.15.refs_0_) | copy-start | bytes 76
  17.4 5.5 %collective-permute-start.1 = (s32[3,2]{1,0:T(4,128)S(1)}, s32[3,2]{1,0:T(4,128)S(1)}, u32[]{:S(2)}, u32[]{:S(2)}) collective-permute-start(s32[3,2]{1,0:T(4,128)S(1)} %copy.15.refs_0_), channel_id=1, source_target_pairs={{0,2},{1,3},{2,4},{3,5},{4,6},{5,7},{6,8},{7,9},{8,10},{9,11},{10,... | collective-permute-start | bytes 80 | tf_op jit(solution)/shard_map/ppermute | solution.py:384
  22.9 0.6 %copy-start.3 = (s32[3,2]{1,0:T(4,128)}, s32[3,2]{1,0:T(4,128)S(1)}, u32[]{:S(2)}) copy-start(s32[3,2]{1,0:T(4,128)S(1)} %collective-permute-done.1.want_ref) | copy-start | bytes 76
  23.5 0.9 %copy-start.1 = (bf16[3,128,1024]{2,1,0:T(8,128)(2,1)}, bf16[3,128,1024]{2,1,0:T(8,128)(2,1)S(1)}, u32[]{:S(2)}) copy-start(bf16[3,128,1024]{2,1,0:T(8,128)(2,1)S(1)} %collective-permute-done.other_ref.refs_6_) | copy-start | bytes 2359300
  26.8 17.9 %collective-permute-start.2 = (bf16[128,1024]{1,0:T(8,128)(2,1)}, bf16[128,1024]{1,0:T(8,128)(2,1)S(1)}, u32[]{:S(2)}, u32[]{:S(2)}) collective-permute-start(bf16[128,1024]{1,0:T(8,128)(2,1)} %chosen_block.1), channel_id=1, source_target_pairs={{2,0},{3,1},{4,2},{5,3},{6,4},{7,5},{8,6},{9,7},{10,8},{11,9},{12,... | collective-permute-start | bytes 786440 | tf_op jit(solution)/shard_map/ppermute | solution.py:392
  30.2 0.7 %copy-start.6 = (bf16[128,1024]{1,0:T(8,128)(2,1)}, bf16[128,1024]{1,0:T(8,128)(2,1)S(1)}, u32[]{:S(2)}) copy-start(bf16[128,1024]{1,0:T(8,128)(2,1)S(1)} %collective-permute-done.4.refs_7_) | copy-start | bytes 786436
  37.4 0.7 %copy-start.5 = (bf16[128,1024]{1,0:T(8,128)(2,1)}, bf16[128,1024]{1,0:T(8,128)(2,1)S(1)}, u32[]{:S(2)}) copy-start(bf16[128,1024]{1,0:T(8,128)(2,1)S(1)} %collective-permute-done.3.refs_7_) | copy-start | bytes 786436
  44.6 0.7 %copy-start.7 = (bf16[128,1024]{1,0:T(8,128)(2,1)}, bf16[128,1024]{1,0:T(8,128)(2,1)S(1)}, u32[]{:S(2)}) copy-start(bf16[128,1024]{1,0:T(8,128)(2,1)S(1)} %collective-permute-done.2.refs_7_) | copy-start | bytes 786436
where the time goes:
time: 52.7 us; the launch traced here: 52.2 us
  Pallas kernels  33.8 us (64%)
  starting transfers between devices  10.3 us (20%)
  local copies, waits for them, and re-layouts  3.67 us (7%)
  waiting for transfers between devices  3.54 us (7%)
  between operations  0.94 us (2%)
    pallas_call x3, Pallas kernels, corr_tile(): pl.pallas_call(functools.partial(corr_kernel, slot, blocks, scale), grid=...  19.7 us
    pallas_call x2, Pallas kernels, spectra(): pl.pallas_call(kernel, grid=(count, 2), out_shape=[jax.ShapeDtypeStruct(s...  11.7 us
    unnamed x17, local copies, waits for them, and re-layouts  3.67 us
    ppermute x1, waiting for transfers between devices, body(): want = lax.ppermute(tile_pairs, 'tile', behind2)  3.53 us
    ppermute x1, starting transfers between devices, body(): far2 = lax.ppermute(pick(want, everything, other), 'tile', ahead2)  3.43 us
    ppermute x1, starting transfers between devices, body(): near1 = lax.ppermute(w1, 'tile', across)  3.12 us
    ppermute x1, starting transfers between devices, body(): far0 = lax.ppermute(w0, 'tile', ahead2)  2.43 us
    pallas_call x1, Pallas kernels, pick(): pl.pallas_call(functools.partial(pick_kernel, blocks), out_shape=jax.Shap...  2.38 us
  transfers between devices with their start and end apart: 5, of which 1 were waited for; matrix products, arithmetic and copies ran while one was open for 0% of the time, Pallas kernels for 29%

commit v1 on v0

v1 whole, which is shorter than its diff:
```python
import functools
import math

import jax
import jax.numpy as jnp
import numpy as np
from jax import lax
from jax.experimental import pallas as pl
from jax.experimental.pallas import tpu as pltpu
from jax.sharding import PartitionSpec as P

CH = 128
WIN = 4096
BAND = 256
BIN0 = 60
SMOOTH = 64
LAGS = 64
ROWS = 16
BF16 = jnp.bfloat16
F32 = jnp.float32


def bin_order():
    return np.concatenate([np.arange(0, BAND, 2), np.arange(1, BAND, 2)])


def dft_tables():
    times = np.arange(WIN // 2, dtype=np.int64)[:, None]
    tables = []
    for parity in range(2):
        freqs = BIN0 + np.arange(parity, BAND, 2, dtype=np.int64)[None, :]
        angle = (times * freqs % WIN) * (2.0 * math.pi / WIN)
        tables.append(np.concatenate([np.cos(angle), -np.sin(angle)], 1))
    return np.stack(tables).astype(BF16)


def mean_table():
    group = bin_order() // SMOOTH
    return ((group[:, None] == group[None, :]) / SMOOTH).astype(BF16)


def phase_tables(coarse, scale):
    fine = LAGS // coarse
    freqs = (BIN0 + bin_order())[None, :]
    lags_a = fine * np.arange(1, coarse // 2 + 1)[:, None]
    lags_b = np.arange(fine)[:, None]
    step = 2.0 * math.pi / WIN
    a = np.concatenate([np.cos(lags_a * freqs * step), np.sin(lags_a * freqs * step)], 1) * scale
    b = np.concatenate([np.cos(lags_b * freqs * step), np.sin(lags_b * freqs * step)], 1)
    return a.astype(np.float32), b.astype(np.float32)


def spectra_kernel(wins, x_ref, mean_ref, tab_ref, w0_ref, w1_ref, all_ref, rows, left, acc):
    m, block = pl.program_id(0), pl.program_id(1)
    for half in range(2):
        rows[half] = x_ref[:, half, 0].reshape(CH * ROWS, 128).astype(F32)
    for s in range(ROWS // wins):
        for w in range(wins):
            first = rows[0, pl.ds(s * wins + w, CH, stride=ROWS), :]
            second = rows[1, pl.ds(s * wins + w, CH, stride=ROWS), :]
            place = (slice(w * CH, (w + 1) * CH), slice(s * 128, (s + 1) * 128))
            left[0, place[0], place[1]] = (first + second).astype(BF16)
            left[1, place[0], place[1]] = (first - second).astype(BF16)
    parts = [
        jnp.dot(left[sign], tab_ref[sign], preferred_element_type=F32) for sign in range(2)
    ]

    @pl.when(m == 0)
    def _():
        for sign in range(2):
            acc[block, sign] = parts[sign]

    @pl.when(m == 1)
    def _():
        spec = [acc[block, sign] + parts[sign] for sign in range(2)]
        energy = [s[:, :128] * s[:, :128] + s[:, 128:] * s[:, 128:] for s in spec]
        energy = jnp.concatenate(energy, 1)
        high = energy.astype(BF16)
        low = (energy - high.astype(F32)).astype(BF16)
        power = jnp.dot(high, mean_ref[...], preferred_element_type=F32)
        power += jnp.dot(low, mean_ref[...], preferred_element_type=F32)
        factor = lax.rsqrt(power + 1e-06)
        for w in range(wins):
            r = slice(w * CH, (w + 1) * CH)
            for q in range(4):
                sign, part = q % 2, q // 2
                value = spec[sign][r, part * 128 : (part + 1) * 128]
                value = value * factor[r, sign * 128 : (sign + 1) * 128]
                column = (w * 4 + q) * 128
                all_ref[block, :, column : column + 128] = value.astype(BF16)

        @pl.when(block == 0)
        def _():
            w0_ref[...] = all_ref[0]

        @pl.when(block == 1)
        def _():
            w1_ref[...] = all_ref[1]


def spectra(view, mean, table, blocks, wins):
    width = WIN // 4
    depth = wins * 2 * BAND
    shapes = [(CH, depth), (CH, depth), (blocks, CH, depth)]
    return pl.pallas_call(
        functools.partial(spectra_kernel, wins),
        grid=(2, blocks),
        out_shape=[jax.ShapeDtypeStruct(shape, BF16) for shape in shapes],
        in_specs=[
            pl.BlockSpec((CH, 2, 1, ROWS, 128), lambda m, b: (b, 0, m, 0, 0)),
            pl.BlockSpec((BAND, BAND), lambda m, b: (0, 0)),
            pl.BlockSpec((2, width, BAND), lambda m, b: (0, m, 0)),
        ],
        out_specs=[pl.BlockSpec(memory_space=pltpu.VMEM)] * len(shapes),
        scratch_shapes=[
            pltpu.VMEM((2, CH * ROWS, 128), F32),
            pltpu.VMEM((2, CH * wins, width), BF16),
            pltpu.VMEM((blocks, 2, CH * wins, BAND), F32),
        ],
        compiler_params=pltpu.CompilerParams(vmem_limit_bytes=60 * 2**20),
        cost_estimate=pl.CostEstimate(
            flops=2 * blocks * CH * wins * WIN * BAND,
            bytes_accessed=2 * blocks * CH * wins * WIN + 2 * WIN * BAND,
            transcendentals=0,
        ),
        name="spectra",
    )(view, mean, table)


def chosen(want, everything, other):
    blocks = everything.shape[0]
    me = lax.axis_index("tile")
    index = want - me * blocks
    own = lax.dynamic_index_in_dim(everything, jnp.clip(index, 0, blocks - 1), 0, keepdims=False)
    beside = lax.dynamic_index_in_dim(
        other, jnp.clip(index + blocks, 0, blocks - 1), 0, keepdims=False
    )
    return jnp.where(jnp.logical_or(index >= 0, me % 2 == 0), own, beside)


def corr_kernel(slot, blocks, scale, coarse, kind, *refs):
    pairs_ref, count_ref, row_ref, atab_ref, btab_ref, all_ref, other_ref, far_ref = refs[:8]
    out_hbm, raw, col, acoef, b0, b1, p0, p1, obuf, in_sem, out_sem = refs[-11:]
    fine = LAGS // coarse
    js = 256 // fine
    chunks = CH // js
    live = count_ref[0] > slot
    me = lax.axis_index("tile")
    index = pairs_ref[slot, 1] - me * blocks
    even = me % 2 == 0
    own = index < blocks
    beside = jnp.logical_and(index >= blocks, jnp.logical_and(even, index < 2 * blocks))
    remote = jnp.logical_not(jnp.logical_or(own, beside))

    def out_copy(c):
        columns = pl.ds(c * js * LAGS, js * LAGS)
        return pltpu.make_async_copy(
            obuf.at[:, columns], out_hbm.at[slot, :, columns], out_sem.at[c]
        )

    @pl.when(live)
    def _():
        @pl.when(own)
        def _():
            pltpu.make_async_copy(all_ref.at[jnp.clip(index, 0, blocks - 1)], raw, in_sem).start()

        @pl.when(beside)
        def _():
            pltpu.make_async_copy(
                other_ref.at[jnp.clip(index - blocks, 0, blocks - 1)], raw, in_sem
            ).start()

        @pl.when(remote)
        def _():
            pltpu.make_async_copy(far_ref, raw, in_sem).start()

        for w in range(2):
            for p in range(2):
                re_cols = slice((w * 4 + p) * 128, (w * 4 + p + 1) * 128)
                im_cols = slice((w * 4 + 2 + p) * 128, (w * 4 + 3 + p) * 128)
                re = row_ref[0, :, re_cols].astype(F32)
                im = row_ref[0, :, im_cols].astype(F32)

                def put(a, re_value, im_value):
                    rows = slice(a * CH, (a + 1) * CH)
                    acoef[rows, re_cols] = re_value.astype(BF16)
                    acoef[rows, im_cols] = im_value.astype(BF16)

                middle = coarse // 2
                put(middle, re * scale, im * scale)
                for n in range(1, middle + 1):
                    cos = atab_ref[n - 1 : n, p * 128 : (p + 1) * 128]
                    sin = atab_ref[n - 1 : n, (2 + p) * 128 : (3 + p) * 128]
                    rc, ic, rs, ims = re * cos, im * cos, re * sin, im * sin
                    put(middle - n, rc + ims, ic - rs)
                    if n < middle:
                        put(middle + n, rc - ims, ic + rs)
        pltpu.make_async_copy(far_ref, raw, in_sem).wait()
        for q in range(8):
            col[q] = raw[:, q * 128 : (q + 1) * 128].astype(F32)

        def build(c, b):
            for w in range(2):
                for p in range(2):
                    re_q, im_q = w * 4 + p, w * 4 + 2 + p
                    cos = btab_ref[:, p * 128 : (p + 1) * 128]
                    sin = btab_ref[:, (2 + p) * 128 : (3 + p) * 128]
                    step = max(ROWS // fine, 1)
                    for place in range(0, js, step):
                        res, ims = [], []
                        for pos in range(place, place + step):
                            v, inner = divmod(pos, 2 * coarse)
                            jj, q = divmod(inner, coarse)
                            j = c * js + v * 2 * coarse + 2 * q + jj
                            re = jnp.concatenate([col[re_q, pl.ds(j, 8, stride=0), :]] * (fine // 8), 0)
                            im = jnp.concatenate([col[im_q, pl.ds(j, 8, stride=0), :]] * (fine // 8), 0)
                            res.append(re * cos + im * sin)
                            ims.append(im * cos - re * sin)
                        rows = slice(place * fine, (place + step) * fine)
                        b[rows, re_q * 128 : (re_q + 1) * 128] = jnp.concatenate(res, 0).astype(BF16)
                        b[rows, im_q * 128 : (im_q + 1) * 128] = jnp.concatenate(ims, 0).astype(BF16)

        def multiply(b, p):
            p[...] = lax.dot_general(
                acoef[...], b[...], (((1,), (1,)), ((), ())), preferred_element_type=F32
            ).astype(kind)

        lane = lax.broadcasted_iota(jnp.int32, (CH, 128), 1)

        def arrange(c, prod):
            for v in range(2):
                x = [prod[a * CH : (a + 1) * CH, v * 128 : (v + 1) * 128] for a in range(coarse)]
                bit = 1
                while bit < coarse:
                    upper = (lane // fine) & bit != 0
                    for a in range(coarse):
                        if a & bit == 0:
                            lo, hi = x[a], x[a | bit]
                            x[a] = jnp.where(upper, pltpu.roll(hi, fine * bit, 1), lo)
                            x[a | bit] = jnp.where(upper, hi, pltpu.roll(lo, 128 - fine * bit, 1))
                    bit *= 2
                for q in range(coarse):
                    column = c * js * LAGS + (v * coarse + q) * 128
                    obuf[:, column : column + 128] = x[q].astype(BF16)
            out_copy(c).start()

        bs, ps = (b0, b1), (p0, p1)
        build(0, b0)
        for c in range(chunks):
            multiply(bs[c % 2], ps[c % 2])
            if c + 1 < chunks:
                build(c + 1, bs[(c + 1) % 2])
            if c > 0:
                arrange(c - 1, ps[(c - 1) % 2])
        arrange(chunks - 1, ps[(chunks - 1) % 2])

    @pl.when(jnp.logical_not(live))
    def _():
        obuf[...] = jnp.zeros_like(obuf)
        for c in range(chunks):
            out_copy(c).start()

    for c in range(chunks):
        out_copy(c).wait()


def corr_tile(slot, scale, coarse, kind, pairs, count, everything, other, far, buffer):
    fine = LAGS // coarse
    tables = [jnp.asarray(t) for t in phase_tables(coarse, scale)]
    js = 256 // fine
    chunks = CH // js
    blocks, _, depth = everything.shape
    in_specs = [
        pl.BlockSpec(memory_space=pltpu.SMEM),
        pl.BlockSpec(memory_space=pltpu.SMEM),
        pl.BlockSpec((1, CH, depth), lambda i: (slot, 0, 0)),
        pl.BlockSpec(memory_space=pltpu.VMEM),
        pl.BlockSpec(memory_space=pltpu.VMEM),
    ] + [pl.BlockSpec(memory_space=pl.ANY)] * 3
    operands = [pairs, count, everything, *tables, everything, other, far]
    aliases = {}
    if buffer is not None:
        aliases = {len(operands): 0}
        operands.append(buffer)
        in_specs.append(pl.BlockSpec(memory_space=pl.ANY))
    return pl.pallas_call(
        functools.partial(corr_kernel, slot, blocks, scale, coarse, kind),
        grid=(1,),
        out_shape=jax.ShapeDtypeStruct((blocks, CH, CH * LAGS), BF16),
        in_specs=in_specs,
        out_specs=pl.BlockSpec(memory_space=pl.ANY),
        scratch_shapes=[
            pltpu.VMEM((CH, depth), BF16),
            pltpu.VMEM((8, CH, 128), F32),
            pltpu.VMEM((coarse * CH, depth), BF16),
            pltpu.VMEM((js * fine, depth), BF16),
            pltpu.VMEM((js * fine, depth), BF16),
            pltpu.VMEM((coarse * CH, js * fine), kind),
            pltpu.VMEM((coarse * CH, js * fine), kind),
            pltpu.VMEM((CH, CH * LAGS), BF16),
            pltpu.SemaphoreType.DMA,
            pltpu.SemaphoreType.DMA((chunks,)),
        ],
        input_output_aliases=aliases,
        compiler_params=pltpu.CompilerParams(vmem_limit_bytes=24 * 2**20),
        cost_estimate=pl.CostEstimate(
            flops=4 * CH * CH * LAGS * depth, bytes_accessed=2 * CH * CH * LAGS, transcendentals=0
        ),
        name=f"lags_{slot}",
    )(*operands)


def body(strain, tile_pairs, tile_count):
    blocks = strain.shape[0] // CH
    wins = strain.shape[1]
    size = lax.axis_size("tile")
    depth = wins * 2 * BAND
    scale = 1.0 / math.sqrt(wins * BAND)
    mean, table = jnp.asarray(mean_table()), jnp.asarray(dft_tables())
    me = lax.axis_index("tile")
    ahead2 = [(i, i - 2) for i in range(2, size)]
    across = [(i, i - 1) for i in range(2, size, 2)]
    swap = [(i, i ^ 1) for i in range(size)]

    view = strain.reshape(blocks * CH, wins, WIN // 128, 128).transpose(0, 2, 1, 3)
    view = view.reshape(blocks * CH, 2, 2, ROWS, 128)
    wants = lax.all_gather(tile_pairs, "tile", tiled=True)
    want = lax.dynamic_index_in_dim(
        wants, jnp.maximum((me - 1) * blocks - 1, 0), 0, keepdims=False
    )[1]
    w0, w1, everything = spectra(view, mean, table, blocks, wins)
    far0 = lax.ppermute(w0, "tile", ahead2)
    near1 = lax.ppermute(w1, "tile", across)
    other = lax.ppermute(everything, "tile", swap)
    far2 = lax.ppermute(chosen(want, everything, other), "tile", ahead2)
    out = None
    forms = ((4, BF16), (2, BF16), (8, F32))
    for slot, far in enumerate((far0, near1, far2)):
        out = corr_tile(
            slot, scale, *forms[slot], tile_pairs, tile_count, everything, other, far, out
        )
    return out


def solution(mesh):
    in_specs = (
        P(("groups", "tile"), None, None),
        P(("groups", "tile"), None),
        P(("groups", "tile")),
    )
    out_specs = P(("groups", "tile"), None, None)
    return jax.shard_map(body, mesh=mesh, in_specs=in_specs, out_specs=out_specs, check_vma=False)
```

time: 52.7 us -> 63.5 us (1.20)
  the two profiles are of different devices: /device:TPU:28 before, /device:TPU:0 now
where the time goes in v1:
time: 63.5 us; the launch traced here: 63.2 us
  Pallas kernels  28.6 us (45%)
  blocking collectives  26.2 us (41%)
  starting transfers between devices  3.7 us (6%)
  local copies, waits for them, and re-layouts  1.95 us (3%)
  between operations  1.66 us (3%)
  other arithmetic  1.01 us (2%)
    all_gather x1, blocking collectives, body(): wants = lax.all_gather(tile_pairs, 'tile', tiled=True)  26.2 us
    pallas_call x3, Pallas kernels, corr_tile(): pl.pallas_call(functools.partial(corr_kernel, slot, blocks, scale, coarse...  17.9 us
    pallas_call x1, Pallas kernels, spectra(): pl.pallas_call(functools.partial(spectra_kernel, wins), grid=(2, blocks),...  10.7 us
    unnamed x18, local copies, waits for them, and re-layouts  1.35 us
    ppermute x1, starting transfers between devices, body(): far2 = lax.ppermute(chosen(want, everything, other), 'tile', ahead2)  1.29 us
    ppermute x1, starting transfers between devices, body(): far0 = lax.ppermute(w0, 'tile', ahead2)  1.28 us
  transfers between devices with their start and end apart: 4, of which 0 were waited for; matrix products, arithmetic and copies ran while one was open for 3% of the time, Pallas kernels for 19%

profile of v1, /device:TPU:0, one launch (start us, length us, event | category | flops | bytes accessed | tf_op | source)
XLA Modules:
  0.0 63.2 jit_solution(6826148955435934859)
XLA Ops:
  0.0 0.0 copy-start.5
  0.0 10.7 %spectra.1 = (bf16[128,1024]{1,0:T(8,128)(2,1)}, bf16[128,1024]{1,0:T(8,128)(2,1)}, bf16[3,128,1024]{2,1,0:T(8,128)(2,1)}) custom-call(bf16[384,2,2,16,128]{4,3,2,1,0:T(8,128)(2,1)} %bitcast.11, bf16[256,256]{1,0:T(8,128)(2,1)} %constant.53.clone.mean_ref, bf16[2,2048,256]{2,1,0:T(8,128)(2,1)} %constant.54.clone.tab_ref), custom_call_target="tpu_custom_call" | custom-call | flops 1610612736 | bytes 8388608 | tf_op jit(solution)/shard_map/spectra/pallas_call | solution.py:105
  10.7 0.5 collective-permute-start
  11.2 1.3 %collective-permute-start.3 = (bf16[128,1024]{1,0:T(8,128)(2,1)}, bf16[128,1024]{1,0:T(8,128)(2,1)S(1)}, u32[]{:S(2)}, u32[]{:S(2)}) collective-permute-start(bf16[128,1024]{1,0:T(8,128)(2,1)} %get-tuple-element.10), channel_id=1, source_target_pairs={{2,0},{3,1},{4,2},{5,3},{6,4},{7,5},{8,6},{9,7},{10,8},{11,9},{12,... | collective-permute-start | bytes 786440 | tf_op jit(solution)/shard_map/ppermute | solution.py:332
  12.5 0.7 %collective-permute-start.2 = (bf16[128,1024]{1,0:T(8,128)(2,1)}, bf16[128,1024]{1,0:T(8,128)(2,1)S(1)}, u32[]{:S(2)}, u32[]{:S(2)}) collective-permute-start(bf16[128,1024]{1,0:T(8,128)(2,1)} %get-tuple-element.9), channel_id=1, source_target_pairs={{2,1},{4,3},{6,5},{8,7},{10,9},{12,11},{14,13},{18,17},{20,19},{22... | collective-permute-start | bytes 786440 | tf_op jit(solution)/shard_map/ppermute | solution.py:333
  13.2 0.0 copy-done.7
  13.2 0.1 copy.28.refs_0_
  13.3 26.2 %all-gather = s32[16,3,2]{1,2,0:T(2,128)S(1)} all-gather(s32[1,3,2]{1,2,0:T(2,128)S(1)} %bitcast.12), channel_id=1, replica_groups=mesh['groups'=2,'tile'=16] {'tile'}, dimensions={0}, use_global_device_ids=true | all-gather | bytes 408 | tf_op jit(solution)/shard_map/all_gather | solution.py:327
  39.5 0.1 reshape.13
  39.6 0.1 constant_dynamic-slice_fusion
  39.7 0.5 slice.4
  41.5 0.0 collective-permute-done.refs_6_
  41.5 0.0 copy-start.1
  41.5 0.0 copy-start.6
  41.5 1.0 %select_bitcast_fusion = bf16[128,1024]{1,0:T(8,128)(2,1)S(1)} fusion(bf16[3,128,1024]{2,1,0:T(8,128)(2,1)S(1)} %collective-permute-done.refs_6_, s32[]{:T(128)S(6)} %min.8, bf16[3,128,1024]{2,1,0:T(8,128)(2,1)} %get-tuple-element.8.refs_2_.refs_5_, s32[]{:T(128)S(6)} %min.7, pred[]{:T(512)S(6)} %or.3), kind=kLoop, calls=%fused_computation | loop fusion | flops 131072 | bytes 786441 | tf_op jit(solution)/shard_map/jit(_where)/select_n | solution.py:138
  42.6 1.3 %collective-permute-start.1 = (bf16[128,1024]{1,0:T(8,128)(2,1)S(1)}, bf16[128,1024]{1,0:T(8,128)(2,1)S(1)}, u32[]{:S(2)}, u32[]{:S(2)}) collective-permute-start(bf16[128,1024]{1,0:T(8,128)(2,1)S(1)} %select_bitcast_fusion), channel_id=1, source_target_pairs={{2,0},{3,1},{4,2},{5,3},{6,4},{7,5},{8,6},{9,7},{10,8},{11,9},{12,... | collective-permute-start | bytes 786440 | tf_op jit(solution)/shard_map/ppermute | solution.py:335
  43.9 0.0 collective-permute-done.3.refs_7_
  43.9 0.0 copy-done.2
  43.9 0.0 copy-done.5
  43.9 0.0 copy-start
  43.9 1.1 %copy-done = bf16[3,128,1024]{2,1,0:T(8,128)(2,1)S(1)} copy-done((bf16[3,128,1024]{2,1,0:T(8,128)(2,1)S(1)}, bf16[3,128,1024]{2,1,0:T(8,128)(2,1)}, u32[]{:S(2)}) %copy-start) | copy-done | bytes 786456
  45.0 5.3 %lags_0.1.refs_8_ = bf16[3,128,8192]{2,1,0:T(8,128)(2,1)} custom-call(s32[3,2]{1,0:T(4,128)S(1)} %copy.28.refs_0_, s32[1]{0:T(128)S(6)} %copy.31.refs_1_, bf16[3,128,1024]{2,1,0:T(8,128)(2,1)S(1)} %copy-done, f32[2,512]{1,0:T(2,128)S(1)} %copy-done.5, f32[16,512]{1,0:T(8,128)S(1)} %copy-done.2, bf16[3,128,1024]{2,1,0:T(8,128)(2,1)S(1)} %copy-done, ...), custom_call_target="tpu_custom_call" | custom-call | flops 4294967296 | bytes 2097152 | tf_op jit(solution)/shard_map/lags_0/pallas_call | solution.py:286
  50.4 0.0 copy-start.3
  50.4 0.0 copy-start.4
  50.4 0.0 collective-permute-done.2.refs_7_
  50.4 0.0 copy-done.1
  50.4 0.0 copy-done.6
  50.4 6.6 %lags_1.1.refs_8_ = bf16[3,128,8192]{2,1,0:T(8,128)(2,1)} custom-call(s32[3,2]{1,0:T(4,128)S(1)} %copy.28.refs_0_, s32[1]{0:T(128)S(6)} %copy.31.refs_1_, bf16[3,128,1024]{2,1,0:T(8,128)(2,1)S(1)} %copy-done, f32[1,512]{1,0:T(1,128)S(1)} %copy-done.6, f32[32,512]{1,0:T(8,128)S(1)} %copy-done.1, ...), custom_call_target="tpu_custom_call", output_to_operand_aliasing={{}: (8, {})} | custom-call | flops 4294967296 | bytes 2097152 | tf_op jit(solution)/shard_map/lags_1/pallas_call | solution.py:286
  57.0 0.0 collective-permute-done.1.refs_7_
  57.1 0.0 copy-done.3
  57.1 0.0 copy-done.4
  57.1 6.0 %lags_2.1 = bf16[3,128,8192]{2,1,0:T(8,128)(2,1)} custom-call(s32[3,2]{1,0:T(4,128)S(1)} %copy.28.refs_0_, s32[1]{0:T(128)S(6)} %copy.31.refs_1_, bf16[3,128,1024]{2,1,0:T(8,128)(2,1)S(1)} %copy-done, f32[4,512]{1,0:T(4,128)S(1)} %copy-done.4, f32[8,512]{1,0:T(8,128)S(1)} %copy-done.3, ...), custom_call_target="tpu_custom_call", output_to_operand_aliasing={{}: (8, {})} | custom-call | flops 4294967296 | bytes 2097152 | tf_op jit(solution)/shard_map/lags_2/pallas_call | solution.py:286
  (3 shorter events, 0.0 us)
Async XLA Ops:
  0.0 43.9 %copy-start.2 = (f32[16,512]{1,0:T(8,128)S(1)}, f32[16,512]{1,0:T(8,128)}, u32[]{:S(2)}) copy-start(f32[16,512]{1,0:T(8,128)} %constant.56.clone.refs_4_) | copy-start | bytes 98308
  0.0 43.9 %copy-start.5 = (f32[2,512]{1,0:T(2,128)S(1)}, f32[2,512]{1,0:T(2,128)}, u32[]{:S(2)}) copy-start(f32[2,512]{1,0:T(2,128)} %constant.55.clone.refs_3_) | copy-start | bytes 12292
  0.0 13.2 %copy-start.7 = (s32[3,2]{0,1:T(2,128)S(1)}, s32[3,2]{0,1:T(2,128)}, u32[]{:S(2)}) copy-start(s32[3,2]{0,1:T(2,128)} %param.12) | copy-start | bytes 76
  10.7 30.8 %collective-permute-start = (bf16[3,128,1024]{2,1,0:T(8,128)(2,1)}, bf16[3,128,1024]{2,1,0:T(8,128)(2,1)S(1)}, u32[]{:S(2)}, u32[]{:S(2)}) collective-permute-start(bf16[3,128,1024]{2,1,0:T(8,128)(2,1)} %get-tuple-element.8.refs_2_.refs_5_), channel_id=1, source_target_pairs={{0,1},{1,0},{2,3},{3,2},{4,5},{5,4},{6,7},{7,6},{8,9},{9,8},{10,11... | collective-permute-start | bytes 2359304 | tf_op jit(solution)/shard_map/ppermute | solution.py:334
  11.2 32.7 %collective-permute-start.3 = (bf16[128,1024]{1,0:T(8,128)(2,1)}, bf16[128,1024]{1,0:T(8,128)(2,1)S(1)}, u32[]{:S(2)}, u32[]{:S(2)}) collective-permute-start(bf16[128,1024]{1,0:T(8,128)(2,1)} %get-tuple-element.10), channel_id=1, source_target_pairs={{2,0},{3,1},{4,2},{5,3},{6,4},{7,5},{8,6},{9,7},{10,8},{11,9},{12,... | collective-permute-start | bytes 786440 | tf_op jit(solution)/shard_map/ppermute | solution.py:332
  12.5 37.9 %collective-permute-start.2 = (bf16[128,1024]{1,0:T(8,128)(2,1)}, bf16[128,1024]{1,0:T(8,128)(2,1)S(1)}, u32[]{:S(2)}, u32[]{:S(2)}) collective-permute-start(bf16[128,1024]{1,0:T(8,128)(2,1)} %get-tuple-element.9), channel_id=1, source_target_pairs={{2,1},{4,3},{6,5},{8,7},{10,9},{12,11},{14,13},{18,17},{20,19},{22... | collective-permute-start | bytes 786440 | tf_op jit(solution)/shard_map/ppermute | solution.py:333
  41.5 8.9 %copy-start.1 = (f32[32,512]{1,0:T(8,128)S(1)}, f32[32,512]{1,0:T(8,128)}, u32[]{:S(2)}) copy-start(f32[32,512]{1,0:T(8,128)} %constant.58.clone.refs_4_) | copy-start | bytes 196612
  41.5 8.9 %copy-start.6 = (f32[1,512]{1,0:T(1,128)S(1)}, f32[1,512]{1,0:T(1,128)}, u32[]{:S(2)}) copy-start(f32[1,512]{1,0:T(1,128)} %constant.57.clone.refs_3_) | copy-start | bytes 6148
  42.6 14.5 %collective-permute-start.1 = (bf16[128,1024]{1,0:T(8,128)(2,1)S(1)}, bf16[128,1024]{1,0:T(8,128)(2,1)S(1)}, u32[]{:S(2)}, u32[]{:S(2)}) collective-permute-start(bf16[128,1024]{1,0:T(8,128)(2,1)S(1)} %select_bitcast_fusion), channel_id=1, source_target_pairs={{2,0},{3,1},{4,2},{5,3},{6,4},{7,5},{8,6},{9,7},{10,8},{11,9},{12,... | collective-permute-start | bytes 786440 | tf_op jit(solution)/shard_map/ppermute | solution.py:335
  43.9 1.1 %copy-start = (bf16[3,128,1024]{2,1,0:T(8,128)(2,1)S(1)}, bf16[3,128,1024]{2,1,0:T(8,128)(2,1)}, u32[]{:S(2)}) copy-start(bf16[3,128,1024]{2,1,0:T(8,128)(2,1)} %get-tuple-element.8.refs_2_.refs_5_) | copy-start | bytes 2359300
  50.4 6.7 %copy-start.3 = (f32[8,512]{1,0:T(8,128)S(1)}, f32[8,512]{1,0:T(8,128)}, u32[]{:S(2)}) copy-start(f32[8,512]{1,0:T(8,128)} %constant.60.clone.refs_4_) | copy-start | bytes 49156
  50.4 6.7 %copy-start.4 = (f32[4,512]{1,0:T(4,128)S(1)}, f32[4,512]{1,0:T(4,128)}, u32[]{:S(2)}) copy-start(f32[4,512]{1,0:T(4,128)} %constant.59.clone.refs_3_) | copy-start | bytes 24580

commit v2 on v1

--- a/solution.py
+++ b/solution.py
@@ -16,6 +16,7 @@
 SMOOTH = 64
 LAGS = 64
 ROWS = 16
+TOGETHER = 8
 BF16 = jnp.bfloat16
 F32 = jnp.float32
 
@@ -50,29 +51,61 @@
     return a.astype(np.float32), b.astype(np.float32)
 
 
-def spectra_kernel(wins, x_ref, mean_ref, tab_ref, w0_ref, w1_ref, all_ref, rows, left, acc):
-    m, block = pl.program_id(0), pl.program_id(1)
+def fold_table(wins):
+    inner = ROWS // wins
+    sign, s, w, c = np.unravel_index(np.arange(256), (2, inner, wins, TOGETHER))
+    table = np.zeros((256, 256), np.float32)
     for half in range(2):
-        rows[half] = x_ref[:, half, 0].reshape(CH * ROWS, 128).astype(F32)
-    for s in range(ROWS // wins):
-        for w in range(wins):
-            first = rows[0, pl.ds(s * wins + w, CH, stride=ROWS), :]
-            second = rows[1, pl.ds(s * wins + w, CH, stride=ROWS), :]
-            place = (slice(w * CH, (w + 1) * CH), slice(s * 128, (s + 1) * 128))
-            left[0, place[0], place[1]] = (first + second).astype(BF16)
-            left[1, place[0], place[1]] = (first - second).astype(BF16)
-    parts = [
-        jnp.dot(left[sign], tab_ref[sign], preferred_element_type=F32) for sign in range(2)
-    ]
-
-    @pl.when(m == 0)
-    def _():
-        for sign in range(2):
-            acc[block, sign] = parts[sign]
-
-    @pl.when(m == 1)
-    def _():
-        spec = [acc[block, sign] + parts[sign] for sign in range(2)]
+        column = np.ravel_multi_index((c, half + 0 * c, s, w), (TOGETHER, 2, inner, wins))
+        table[np.arange(256), column] = np.where((sign == 1) & (half == 1), -1.0, 1.0)
+    return table.astype(BF16)
+
+
+def spectra_kernel(wins, x_ref, fold_ref, mean_ref, tab_hbm, w0_ref, w1_ref, all_ref, tab, left, sem):
+    block, side = pl.program_id(0), pl.program_id(1)
+    part = CH // 2
+    start = jnp.logical_and(block == 0, side == 0)
+
+    @pl.when(start)
+    def _():
+        pltpu.make_async_copy(tab_hbm, tab, sem).start()
+
+    for m in range(2):
+        for first in range(0, part // TOGETHER, 4):
+            groups = []
+            for g in range(first, first + 4):
+                rows = x_ref[g * TOGETHER : (g + 1) * TOGETHER, :, m]
+                groups.append(rows.reshape(TOGETHER * 2 * ROWS, 128))
+            folded = jnp.dot(
+                fold_ref[...], jnp.concatenate(groups, 1), preferred_element_type=F32
+            )
+            for sign in range(2):
+                for s in range(ROWS // wins):
+                    for w in range(wins):
+                        row = ((sign * (ROWS // wins) + s) * wins + w) * TOGETHER
+                        for n in range(0, 4, 2):
+                            pair = [
+                                folded[row : row + TOGETHER, k * 128 : (k + 1) * 128]
+                                for k in (n, n + 1)
+                            ]
+                            to = w * part + (first + n) * TOGETHER
+                            column = (m * (ROWS // wins) + s) * 128
+                            left[sign, side, to : to + 2 * TOGETHER, column : column + 128] = (
+                                jnp.concatenate(pair, 0).astype(BF16)
+                            )
+
+    @pl.when(jnp.logical_and(block == 0, side == 1))
+    def _():
+        pltpu.make_async_copy(tab_hbm, tab, sem).wait()
+
+    @pl.when(side == 1)
+    def _():
+        spec = [
+            jnp.dot(
+                left[sign].reshape(CH * wins, WIN // 2), tab[sign], preferred_element_type=F32
+            )
+            for sign in range(2)
+        ]
         energy = [s[:, :128] * s[:, :128] + s[:, 128:] * s[:, 128:] for s in spec]
         energy = jnp.concatenate(energy, 1)
         high = energy.astype(BF16)
@@ -80,14 +113,17 @@
         power = jnp.dot(high, mean_ref[...], preferred_element_type=F32)
         power += jnp.dot(low, mean_ref[...], preferred_element_type=F32)
         factor = lax.rsqrt(power + 1e-06)
-        for w in range(wins):
-            r = slice(w * CH, (w + 1) * CH)
-            for q in range(4):
-                sign, part = q % 2, q // 2
-                value = spec[sign][r, part * 128 : (part + 1) * 128]
-                value = value * factor[r, sign * 128 : (sign + 1) * 128]
-                column = (w * 4 + q) * 128
-                all_ref[block, :, column : column + 128] = value.astype(BF16)
+        for h in range(2):
+            for w in range(wins):
+                r = slice((h * wins + w) * part, (h * wins + w + 1) * part)
+                for q in range(4):
+                    sign, half = q % 2, q // 2
+                    value = spec[sign][r, half * 128 : (half + 1) * 128]
+                    value = value * factor[r, sign * 128 : (sign + 1) * 128]
+                    column = (w * 4 + q) * 128
+                    all_ref[block, h * part : (h + 1) * part, column : column + 128] = (
+                        value.astype(BF16)
+                    )
 
         @pl.when(block == 0)
         def _():
@@ -98,24 +134,24 @@
             w1_ref[...] = all_ref[1]
 
 
-def spectra(view, mean, table, blocks, wins):
-    width = WIN // 4
+def spectra(view, fold, mean, table, blocks, wins):
     depth = wins * 2 * BAND
     shapes = [(CH, depth), (CH, depth), (blocks, CH, depth)]
     return pl.pallas_call(
         functools.partial(spectra_kernel, wins),
-        grid=(2, blocks),
+        grid=(blocks, 2),
         out_shape=[jax.ShapeDtypeStruct(shape, BF16) for shape in shapes],
         in_specs=[
-            pl.BlockSpec((CH, 2, 1, ROWS, 128), lambda m, b: (b, 0, m, 0, 0)),
-            pl.BlockSpec((BAND, BAND), lambda m, b: (0, 0)),
-            pl.BlockSpec((2, width, BAND), lambda m, b: (0, m, 0)),
+            pl.BlockSpec((CH // 2, 2, 2, ROWS, 128), lambda b, h: (2 * b + h, 0, 0, 0, 0)),
+            pl.BlockSpec((256, 256), lambda b, h: (0, 0)),
+            pl.BlockSpec((BAND, BAND), lambda b, h: (0, 0)),
+            pl.BlockSpec(memory_space=pl.ANY),
         ],
         out_specs=[pl.BlockSpec(memory_space=pltpu.VMEM)] * len(shapes),
         scratch_shapes=[
-            pltpu.VMEM((2, CH * ROWS, 128), F32),
-            pltpu.VMEM((2, CH * wins, width), BF16),
-            pltpu.VMEM((blocks, 2, CH * wins, BAND), F32),
+            pltpu.VMEM((2, WIN // 2, BAND), BF16),
+            pltpu.VMEM((2, 2, CH // 2 * wins, WIN // 2), BF16),
+            pltpu.SemaphoreType.DMA,
         ],
         compiler_params=pltpu.CompilerParams(vmem_limit_bytes=60 * 2**20),
         cost_estimate=pl.CostEstimate(
@@ -124,7 +160,7 @@
             transcendentals=0,
         ),
         name="spectra",
-    )(view, mean, table)
+    )(view, fold, mean, table)
 
 
 def chosen(want, everything, other):
@@ -248,10 +284,10 @@
         build(0, b0)
         for c in range(chunks):
             multiply(bs[c % 2], ps[c % 2])
+            if c > 0:
+                arrange(c - 1, ps[(c - 1) % 2])
             if c + 1 < chunks:
                 build(c + 1, bs[(c + 1) % 2])
-            if c > 0:
-                arrange(c - 1, ps[(c - 1) % 2])
         arrange(chunks - 1, ps[(chunks - 1) % 2])
 
     @pl.when(jnp.logical_not(live))
@@ -316,25 +352,21 @@
     size = lax.axis_size("tile")
     depth = wins * 2 * BAND
     scale = 1.0 / math.sqrt(wins * BAND)
-    mean, table = jnp.asarray(mean_table()), jnp.asarray(dft_tables())
-    me = lax.axis_index("tile")
+    fold, mean, table = [jnp.asarray(t) for t in (fold_table(wins), mean_table(), dft_tables())]
     ahead2 = [(i, i - 2) for i in range(2, size)]
     across = [(i, i - 1) for i in range(2, size, 2)]
     swap = [(i, i ^ 1) for i in range(size)]
 
     view = strain.reshape(blocks * CH, wins, WIN // 128, 128).transpose(0, 2, 1, 3)
     view = view.reshape(blocks * CH, 2, 2, ROWS, 128)
-    wants = lax.all_gather(tile_pairs, "tile", tiled=True)
-    want = lax.dynamic_index_in_dim(
-        wants, jnp.maximum((me - 1) * blocks - 1, 0), 0, keepdims=False
-    )[1]
-    w0, w1, everything = spectra(view, mean, table, blocks, wins)
+    want = lax.ppermute(tile_pairs, "tile", [(i, i + 2) for i in range(size - 2)])
+    w0, w1, everything = spectra(view, fold, mean, table, blocks, wins)
     far0 = lax.ppermute(w0, "tile", ahead2)
     near1 = lax.ppermute(w1, "tile", across)
     other = lax.ppermute(everything, "tile", swap)
-    far2 = lax.ppermute(chosen(want, everything, other), "tile", ahead2)
+    far2 = lax.ppermute(chosen(want[blocks - 1, 1], everything, other), "tile", ahead2)
     out = None
-    forms = ((4, BF16), (2, BF16), (8, F32))
+    forms = ((4, F32), (8, F32), (4, F32))
     for slot, far in enumerate((far0, near1, far2)):
         out = corr_tile(
             slot, scale, *forms[slot], tile_pairs, tile_count, everything, other, far, out

time: 63.5 us -> 44.1 us (0.69)
  the two profiles are of different devices: /device:TPU:0 before, /device:TPU:30 now
where the time goes in v2:
time: 44.1 us; the launch traced here: 43.8 us
  Pallas kernels  27.2 us (62%)
  starting transfers between devices  12.1 us (27%)
  local copies, waits for them, and re-layouts  1.86 us (4%)
  between operations  1.67 us (4%)
  other arithmetic  0.99 us (2%)
    pallas_call x3, Pallas kernels, corr_tile(): pl.pallas_call(functools.partial(corr_kernel, slot, blocks, scale, coarse...  16.7 us
    pallas_call x1, Pallas kernels, spectra(): pl.pallas_call(functools.partial(spectra_kernel, wins), grid=(blocks, 2),...  10.5 us
    ppermute x1, starting transfers between devices, body(): lax.ppermute(chosen(want[blocks - 1, 1], everything, other), 'tile', ahead2)  4.21 us
    ppermute x1, starting transfers between devices, body(): near1 = lax.ppermute(w1, 'tile', across)  4.09 us
    ppermute x1, starting transfers between devices, body(): far0 = lax.ppermute(w0, 'tile', ahead2)  2.43 us
    ppermute x1, starting transfers between devices, body(): lax.ppermute(tile_pairs, 'tile', [(i, i + 2) for i in range(size - 2)])  1.29 us
    unnamed x13, local copies, waits for them, and re-layouts  1.25 us
    select_n x1, other arithmetic, chosen(): return jnp.where(jnp.logical_or(index >= 0, me % 2 == 0), own, beside)  0.99 us
  transfers between devices with their start and end apart: 5, of which 0 were waited for; matrix products, arithmetic and copies ran while one was open for 4% of the time, Pallas kernels for 25%

profile of v2, /device:TPU:30, one launch (start us, length us, event | category | flops | bytes accessed | tf_op | source)
XLA Modules:
  0.0 43.8 jit_solution(10333909711969748281)
XLA Ops:
  0.0 0.0 copy-start.1
  0.0 0.0 copy-start.4
  0.0 0.0 copy-start.5
  0.0 10.5 %spectra.1 = (bf16[128,1024]{1,0:T(8,128)(2,1)}, bf16[128,1024]{1,0:T(8,128)(2,1)}, bf16[3,128,1024]{2,1,0:T(8,128)(2,1)}) custom-call(bf16[384,2,2,16,128]{4,3,2,1,0:T(8,128)(2,1)} %bitcast.8, bf16[256,256]{1,0:T(8,128)(2,1)} %constant.42.clone.fold_ref, bf16[256,256]{1,0:T(8,128)(2,1)} %constant.43.clone.mean_ref, bf16[2,2048,256]{2,1,0:T(8,128)(2,1)} %constant.44.clone.tab_hbm), custom_call_target="tpu_custom_call" | custom-call | flops 1610612736 | bytes 8388608 | tf_op jit(solution)/shard_map/spectra/pallas_call | solution.py:140
  10.5 0.1 collective-permute-start
  10.6 2.4 %collective-permute-start.4 = (bf16[128,1024]{1,0:T(8,128)(2,1)}, bf16[128,1024]{1,0:T(8,128)(2,1)S(1)}, u32[]{:S(2)}, u32[]{:S(2)}) collective-permute-start(bf16[128,1024]{1,0:T(8,128)(2,1)} %get-tuple-element.10), channel_id=1, source_target_pairs={{2,0},{3,1},{4,2},{5,3},{6,4},{7,5},{8,6},{9,7},{10,8},{11,9},{12,... | collective-permute-start | bytes 786440 | tf_op jit(solution)/shard_map/ppermute | solution.py:364
  13.0 0.0 copy-done.5
  13.0 1.3 %collective-permute-start.1 = (s32[3,2]{0,1:T(2,128)S(1)}, s32[3,2]{0,1:T(2,128)S(1)}, u32[]{:S(2)}, u32[]{:S(2)}) collective-permute-start(s32[3,2]{0,1:T(2,128)S(1)} %copy-done.5), channel_id=1, source_target_pairs={{0,2},{1,3},{2,4},{3,5},{4,6},{5,7},{6,8},{7,9},{8,10},{9,11},{10,... | collective-permute-start | bytes 80 | tf_op jit(solution)/shard_map/ppermute | solution.py:362
  14.3 4.1 %collective-permute-start.3 = (bf16[128,1024]{1,0:T(8,128)(2,1)}, bf16[128,1024]{1,0:T(8,128)(2,1)S(1)}, u32[]{:S(2)}, u32[]{:S(2)}) collective-permute-start(bf16[128,1024]{1,0:T(8,128)(2,1)} %get-tuple-element.9), channel_id=1, source_target_pairs={{2,1},{4,3},{6,5},{8,7},{10,9},{12,11},{14,13},{18,17},{20,19},{22... | collective-permute-start | bytes 786440 | tf_op jit(solution)/shard_map/ppermute | solution.py:365
  18.4 0.1 copy.18.refs_0_
  19.2 0.0 collective-permute-done.1
  19.2 0.6 %slice.3 = s32[1,1]{0,1:T(1,128)} slice(s32[3,2]{0,1:T(2,128)S(1)} %collective-permute-done.1), slice={[2:3], [1:2]} | slice | bytes 8 | tf_op jit(solution)/shard_map/slice | solution.py:367
  20.4 0.0 collective-permute-done.refs_6_
  20.5 0.0 copy-start.2
  20.5 0.0 copy-start.3
  20.5 1.0 %select_bitcast_fusion = bf16[128,1024]{1,0:T(8,128)(2,1)S(1)} fusion(bf16[3,128,1024]{2,1,0:T(8,128)(2,1)S(1)} %collective-permute-done.refs_6_, s32[]{:T(128)S(6)} %min.8, bf16[3,128,1024]{2,1,0:T(8,128)(2,1)} %get-tuple-element.8.refs_2_.refs_5_, s32[]{:T(128)S(6)} %min.7, pred[]{:T(512)S(6)} %or.3), kind=kLoop, calls=%fused_computation | loop fusion | flops 131072 | bytes 786441 | tf_op jit(solution)/shard_map/jit(_where)/select_n | solution.py:174
  21.5 4.2 %collective-permute-start.2 = (bf16[128,1024]{1,0:T(8,128)(2,1)S(1)}, bf16[128,1024]{1,0:T(8,128)(2,1)S(1)}, u32[]{:S(2)}, u32[]{:S(2)}) collective-permute-start(bf16[128,1024]{1,0:T(8,128)(2,1)S(1)} %select_bitcast_fusion), channel_id=1, source_target_pairs={{2,0},{3,1},{4,2},{5,3},{6,4},{7,5},{8,6},{9,7},{10,8},{11,9},{12,... | collective-permute-start | bytes 786440 | tf_op jit(solution)/shard_map/ppermute | solution.py:367
  25.7 0.0 collective-permute-done.4.refs_7_
  25.7 0.0 copy-done.1
  25.7 0.0 copy-done.4
  25.7 0.0 copy-start
  25.7 1.1 %copy-done = bf16[3,128,1024]{2,1,0:T(8,128)(2,1)S(1)} copy-done((bf16[3,128,1024]{2,1,0:T(8,128)(2,1)S(1)}, bf16[3,128,1024]{2,1,0:T(8,128)(2,1)}, u32[]{:S(2)}) %copy-start) | copy-done | bytes 786456
  26.9 5.4 %lags_0.1.refs_8_ = bf16[3,128,8192]{2,1,0:T(8,128)(2,1)} custom-call(s32[3,2]{1,0:T(4,128)S(1)} %copy.18.refs_0_, s32[1]{0:T(128)S(6)} %copy.21.refs_1_, bf16[3,128,1024]{2,1,0:T(8,128)(2,1)S(1)} %copy-done, f32[2,512]{1,0:T(2,128)S(1)} %copy-done.4, f32[16,512]{1,0:T(8,128)S(1)} %copy-done.1, bf16[3,128,1024]{2,1,0:T(8,128)(2,1)S(1)} %copy-done, ...), custom_call_target="tpu_custom_call" | custom-call | flops 4294967296 | bytes 2097152 | tf_op jit(solution)/shard_map/lags_0/pallas_call | solution.py:322
  32.2 0.0 collective-permute-done.3.refs_7_
  32.2 0.0 copy-done.2
  32.2 0.0 copy-done.3
  32.3 5.8 %lags_1.1.refs_8_ = bf16[3,128,8192]{2,1,0:T(8,128)(2,1)} custom-call(s32[3,2]{1,0:T(4,128)S(1)} %copy.18.refs_0_, s32[1]{0:T(128)S(6)} %copy.21.refs_1_, bf16[3,128,1024]{2,1,0:T(8,128)(2,1)S(1)} %copy-done, f32[4,512]{1,0:T(4,128)S(1)} %copy-done.3, f32[8,512]{1,0:T(8,128)S(1)} %copy-done.2, ...), custom_call_target="tpu_custom_call", output_to_operand_aliasing={{}: (8, {})} | custom-call | flops 4294967296 | bytes 2097152 | tf_op jit(solution)/shard_map/lags_1/pallas_call | solution.py:322
  38.1 0.0 collective-permute-done.2.refs_7_
  38.1 5.5 %lags_2.1 = bf16[3,128,8192]{2,1,0:T(8,128)(2,1)} custom-call(s32[3,2]{1,0:T(4,128)S(1)} %copy.18.refs_0_, s32[1]{0:T(128)S(6)} %copy.21.refs_1_, bf16[3,128,1024]{2,1,0:T(8,128)(2,1)S(1)} %copy-done, f32[2,512]{1,0:T(2,128)S(1)} %copy-done.4, f32[16,512]{1,0:T(8,128)S(1)} %copy-done.1, ...), custom_call_target="tpu_custom_call", output_to_operand_aliasing={{}: (8, {})} | custom-call | flops 4294967296 | bytes 2097152 | tf_op jit(solution)/shard_map/lags_2/pallas_call | solution.py:322
Async XLA Ops:
  0.0 25.7 %copy-start.1 = (f32[16,512]{1,0:T(8,128)S(1)}, f32[16,512]{1,0:T(8,128)}, u32[]{:S(2)}) copy-start(f32[16,512]{1,0:T(8,128)} %constant.46.clone.refs_4_) | copy-start | bytes 98308
  0.0 25.7 %copy-start.4 = (f32[2,512]{1,0:T(2,128)S(1)}, f32[2,512]{1,0:T(2,128)}, u32[]{:S(2)}) copy-start(f32[2,512]{1,0:T(2,128)} %constant.45.clone.refs_3_) | copy-start | bytes 12292
  0.0 13.0 %copy-start.5 = (s32[3,2]{0,1:T(2,128)S(1)}, s32[3,2]{0,1:T(2,128)}, u32[]{:S(2)}) copy-start(s32[3,2]{0,1:T(2,128)} %param.13) | copy-start | bytes 76
  10.5 10.0 %collective-permute-start = (bf16[3,128,1024]{2,1,0:T(8,128)(2,1)}, bf16[3,128,1024]{2,1,0:T(8,128)(2,1)S(1)}, u32[]{:S(2)}, u32[]{:S(2)}) collective-permute-start(bf16[3,128,1024]{2,1,0:T(8,128)(2,1)} %get-tuple-element.8.refs_2_.refs_5_), channel_id=1, source_target_pairs={{0,1},{1,0},{2,3},{3,2},{4,5},{5,4},{6,7},{7,6},{8,9},{9,8},{10,11... | collective-permute-start | bytes 2359304 | tf_op jit(solution)/shard_map/ppermute | solution.py:366
  10.6 15.1 %collective-permute-start.4 = (bf16[128,1024]{1,0:T(8,128)(2,1)}, bf16[128,1024]{1,0:T(8,128)(2,1)S(1)}, u32[]{:S(2)}, u32[]{:S(2)}) collective-permute-start(bf16[128,1024]{1,0:T(8,128)(2,1)} %get-tuple-element.10), channel_id=1, source_target_pairs={{2,0},{3,1},{4,2},{5,3},{6,4},{7,5},{8,6},{9,7},{10,8},{11,9},{12,... | collective-permute-start | bytes 786440 | tf_op jit(solution)/shard_map/ppermute | solution.py:364
  13.0 6.2 %collective-permute-start.1 = (s32[3,2]{0,1:T(2,128)S(1)}, s32[3,2]{0,1:T(2,128)S(1)}, u32[]{:S(2)}, u32[]{:S(2)}) collective-permute-start(s32[3,2]{0,1:T(2,128)S(1)} %copy-done.5), channel_id=1, source_target_pairs={{0,2},{1,3},{2,4},{3,5},{4,6},{5,7},{6,8},{7,9},{8,10},{9,11},{10,... | collective-permute-start | bytes 80 | tf_op jit(solution)/shard_map/ppermute | solution.py:362
  14.3 17.9 %collective-permute-start.3 = (bf16[128,1024]{1,0:T(8,128)(2,1)}, bf16[128,1024]{1,0:T(8,128)(2,1)S(1)}, u32[]{:S(2)}, u32[]{:S(2)}) collective-permute-start(bf16[128,1024]{1,0:T(8,128)(2,1)} %get-tuple-element.9), channel_id=1, source_target_pairs={{2,1},{4,3},{6,5},{8,7},{10,9},{12,11},{14,13},{18,17},{20,19},{22... | collective-permute-start | bytes 786440 | tf_op jit(solution)/shard_map/ppermute | solution.py:365
  20.5 11.8 %copy-start.2 = (f32[8,512]{1,0:T(8,128)S(1)}, f32[8,512]{1,0:T(8,128)}, u32[]{:S(2)}) copy-start(f32[8,512]{1,0:T(8,128)} %constant.48.clone.refs_4_) | copy-start | bytes 49156
  20.5 11.8 %copy-start.3 = (f32[4,512]{1,0:T(4,128)S(1)}, f32[4,512]{1,0:T(4,128)}, u32[]{:S(2)}) copy-start(f32[4,512]{1,0:T(4,128)} %constant.47.clone.refs_3_) | copy-start | bytes 24580
  21.5 16.6 %collective-permute-start.2 = (bf16[128,1024]{1,0:T(8,128)(2,1)S(1)}, bf16[128,1024]{1,0:T(8,128)(2,1)S(1)}, u32[]{:S(2)}, u32[]{:S(2)}) collective-permute-start(bf16[128,1024]{1,0:T(8,128)(2,1)S(1)} %select_bitcast_fusion), channel_id=1, source_target_pairs={{2,0},{3,1},{4,2},{5,3},{6,4},{7,5},{8,6},{9,7},{10,8},{11,9},{12,... | collective-permute-start | bytes 786440 | tf_op jit(solution)/shard_map/ppermute | solution.py:367
  25.7 1.1 %copy-start = (bf16[3,128,1024]{2,1,0:T(8,128)(2,1)S(1)}, bf16[3,128,1024]{2,1,0:T(8,128)(2,1)}, u32[]{:S(2)}) copy-start(bf16[3,128,1024]{2,1,0:T(8,128)(2,1)} %get-tuple-element.8.refs_2_.refs_5_) | copy-start | bytes 2359300
